TPU v7x, 128 devices: a whole 4x4x4 slice. The times are simulated.
128 devices in a mesh: cls: 16 (over y, z_hi, core), feat: 8 (over z_lo, x).
Axes of the slice: x: 4, y: 4, z: 4 (z_hi: 2, z_lo: 2; z = z_hi * 2 + z_lo), core: 2. Of those that a mesh axis runs over, the one named last changes fastest.
Arguments:
- embeddings: bfloat16 [16384, 4608], P(('cls', 'feat')), may hold values from -6 to 6
- labels: int32 [16384, 1], P(('cls', 'feat')), may hold values from 0 to 15; in each aligned block of 128 rows (0 to 127, 128 to 255, ...) at most 16 rows name the same one
- previous: float32 [16, 4608, 1152], P('cls', 'feat'), as said below
Outputs:
- class_cov: float32 [16, 4608, 4608], P('cls', None, 'feat')
- panel_factor: float32 [16, 4608, 1152], P('cls', 'feat')
Inputs may be any that keep to these rules, and one draw needn't show every extreme that they name: `labels`: among the rows of one device no class has more than 16 rows, and on every device some class has exactly 16; every class has a row somewhere. For every class the first 1152 rows of previous form a symmetric positive definite matrix whose smallest eigenvalue is at least 0.05.
All inputs are finite; a program needn't handle non-finite values.
Results may differ from a plain program's by a relative error of at most 0.0003.
Values may be sent and summed in bfloat16 or wider, within the bound.
A program may use at most 192 MiB of HBM per device.

v0:
```python
import jax
import jax.numpy as jnp
from jax import lax
from jax.sharding import PartitionSpec as P


def from_root(value, axis, root):
    mine = lax.axis_index(axis) == root
    return lax.psum(jnp.where(mine, value, jnp.zeros_like(value)), axis)


def body(embeddings, labels, previous):
    rows_dev = embeddings.shape[0]
    width = embeddings.shape[1]
    classes = lax.axis_size("cls")
    feat_count = lax.axis_size("feat")
    capacity = 2 * rows_dev // classes
    tile_width = width // feat_count
    col_start = lax.axis_index("feat") * tile_width
    label_col = labels[:, 0]
    onehot = (label_col[:, None] == jnp.arange(classes, dtype=jnp.int32)[None, :]).astype(jnp.int32)
    ranks = jnp.sum((jnp.cumsum(onehot, axis=0) - 1) * onehot, axis=1)
    counts = jnp.sum(onehot, axis=0).reshape(classes, 1)
    buffer = (
        jnp.zeros((classes, capacity, width), jnp.bfloat16).at[label_col, ranks].set(embeddings)
    )
    rows_part = lax.all_to_all(
        jnp.repeat(buffer, feat_count, axis=0),
        ("cls", "feat"),
        split_axis=0,
        concat_axis=0,
        tiled=True,
    )
    count_part = lax.all_to_all(
        jnp.repeat(counts, feat_count, axis=0),
        ("cls", "feat"),
        split_axis=0,
        concat_axis=0,
        tiled=True,
    )
    flattened = rows_part.reshape(-1, width)
    tile_cols = lax.dynamic_slice_in_dim(flattened, col_start, tile_width, 1)
    gram = lax.dot_general(
        flattened, tile_cols, (((0,), (0,)), ((), ())), preferred_element_type=jnp.float32
    )
    sums = jnp.sum(flattened, axis=0, dtype=jnp.float32)
    total = jnp.sum(count_part).astype(jnp.float32)
    gram, sums, total = (gram, sums, total)
    mean = sums / total
    mean_tile = lax.dynamic_slice_in_dim(mean, col_start, tile_width, 0)
    class_cov = gram / total - mean[:, None] * mean_tile[None, :]
    local_rows = previous.shape[1]
    panel = previous.shape[2]
    pieces = []
    for source in range(panel // local_rows):
        pieces.append(from_root(previous[0], "feat", source))
    leading = jnp.concatenate(pieces, axis=0)
    lower_factor = jnp.linalg.cholesky(leading)
    factor_rows = lax.linalg.triangular_solve(
        lower_factor, previous[0], left_side=False, lower=True, transpose_a=True
    )
    return (class_cov[None], factor_rows[None])


def solution(mesh):
    return jax.shard_map(
        body,
        mesh=mesh,
        in_specs=(P(("cls", "feat"), None), P(("cls", "feat"), None), P("cls", "feat", None)),
        out_specs=(P("cls", None, "feat"), P("cls", "feat", None)),
        check_vma=False,
    )
```

profile of v0, /device:TPU:119, one launch (start us, length us, event | category | flops | bytes accessed | tf_op | source)
XLA Modules:
  0.0 799.5 jit_solution(1845885607561038181)
XLA Ops:
  15.3 10.5 %all-to-all-start.1 = ((s32[128,1,1]{2,1,0:T(1,128)}), s32[128,1,1]{2,1,0:T(1,128)}, u32[]{:S(2)}, u32[]{:S(2)}) async-start(s32[128,1,1]{2,1,0:T(1,128)} %broadcast_in_dim.30), calls=%async_computation.1 | async-start | bytes 131072 | tf_op jit(solution)/shard_map/all_to_all | solution.py:34
  26.1 21.4 %scatter_fusion = bf16[16,16,4608]{2,1,0:T(8,128)(2,1)S(1)} fusion(bf16[16,16,4608]{2,1,0:T(8,128)(2,1)S(1)} %broadcast_in_dim.24, s32[128]{0:T(128)S(1)} %fusion.81, bf16[128,4608]{1,0:T(8,128)(2,1)S(1)} %copy-done.4), kind=kCustom, calls=%fused_computation | custom fusion | bytes 3539968 | tf_op jit(solution)/shard_map/scatter | solution.py:25
  47.5 6.9 broadcast_in_dim.25
  54.4 10.2 %all-to-all-start = ((bf16[128,16,4608]{2,1,0:T(8,128)(2,1)}), bf16[128,16,4608]{2,1,0:T(8,128)(2,1)}, u32[]{:S(2)}, u32[]{:S(2)}) async-start(bf16[128,16,4608]{2,1,0:T(8,128)(2,1)} %bitcast.136), calls=%async_computation | async-start | bytes 37748736 | tf_op jit(solution)/shard_map/all_to_all | solution.py:27
  66.9 288.2 %all-reduce.4.cloned.1.call-done = (f32[576,1152]{0,1:T(8,128)}, f32[576,1152]{0,1:T(8,128)}) async-done(((f32[576,1152]{0,1:T(8,128)}, f32[576,1152]{0,1:T(8,128)}), (f32[576,1152]{0,1:T(8,128)}, f32[576,1152]{0,1:T(8,128)})) %all-reduce.4.cloned.1.call-update) | async-done | bytes 5308432 | tf_op jit(solution)/shard_map/psum | solution.py:9
  355.1 6.0 pad_maximum_fusion
  361.1 7.2 copy.22
  368.3 4.4 fusion
  375.0 11.7 %cholesky.251 = f32[128,128]{1,0:T(8,128)S(1)} custom-call(f32[128,128]{1,0:T(8,128)S(1)} %cholesky.658), custom_call_target="Cholesky" | custom-call | tf_op jit(solution)/shard_map/jit(cholesky)/cholesky | solution.py:58
  386.8 9.8 %custom-call.70 = f32[1,128,128]{1,2,0:T(8,128)S(1)} custom-call(f32[1,128,128]{2,1,0:T(8,128)S(1)} %get-tuple-element.84), custom_call_target="InvertDiagBlocksLowerTriangular" | custom-call | tf_op jit(solution)/shard_map/jit(cholesky)/cholesky | solution.py:58
  403.4 12.1 %cholesky.274 = f32[128,128]{1,0:T(8,128)S(1)} custom-call(f32[128,128]{1,0:T(8,128)S(1)} %cholesky.662), custom_call_target="Cholesky" | custom-call | tf_op jit(solution)/shard_map/jit(cholesky)/cholesky | solution.py:58
  416.1 9.8 %custom-call.71 = f32[1,128,128]{1,2,0:T(8,128)S(1)} custom-call(f32[1,128,128]{2,1,0:T(8,128)S(1)} %get-tuple-element.81), custom_call_target="InvertDiagBlocksLowerTriangular" | custom-call | tf_op jit(solution)/shard_map/jit(cholesky)/cholesky | solution.py:58
  429.5 11.7 %cholesky.525 = f32[128,128]{1,0:T(8,128)S(1)} custom-call(f32[128,128]{1,0:T(8,128)S(1)} %cholesky.667), custom_call_target="Cholesky" | custom-call | tf_op jit(solution)/shard_map/jit(cholesky)/cholesky | solution.py:58
  441.8 9.8 %custom-call.72 = f32[1,128,128]{1,2,0:T(8,128)S(1)} custom-call(f32[1,128,128]{2,1,0:T(8,128)S(1)} %get-tuple-element.78), custom_call_target="InvertDiagBlocksLowerTriangular" | custom-call | tf_op jit(solution)/shard_map/jit(cholesky)/cholesky | solution.py:58
  455.5 11.9 %cholesky.544 = f32[128,128]{1,0:T(8,128)S(1)} custom-call(f32[128,128]{1,0:T(8,128)S(1)} %cholesky.672), custom_call_target="Cholesky" | custom-call | tf_op jit(solution)/shard_map/jit(cholesky)/cholesky | solution.py:58
  468.0 9.8 %custom-call.73 = f32[1,128,128]{1,2,0:T(8,128)S(1)} custom-call(f32[1,128,128]{2,1,0:T(8,128)S(1)} %get-tuple-element.75), custom_call_target="InvertDiagBlocksLowerTriangular" | custom-call | tf_op jit(solution)/shard_map/jit(cholesky)/cholesky | solution.py:58
  481.6 11.7 %cholesky.563 = f32[128,128]{1,0:T(8,128)S(1)} custom-call(f32[128,128]{1,0:T(8,128)S(1)} %cholesky.677), custom_call_target="Cholesky" | custom-call | tf_op jit(solution)/shard_map/jit(cholesky)/cholesky | solution.py:58
  493.9 10.0 %custom-call.74 = f32[1,128,128]{1,2,0:T(8,128)S(1)} custom-call(f32[1,128,128]{2,1,0:T(8,128)S(1)} %get-tuple-element.72), custom_call_target="InvertDiagBlocksLowerTriangular" | custom-call | tf_op jit(solution)/shard_map/jit(cholesky)/cholesky | solution.py:58
  507.7 11.7 %cholesky.583 = f32[128,128]{1,0:T(8,128)S(1)} custom-call(f32[128,128]{1,0:T(8,128)S(1)} %cholesky.682), custom_call_target="Cholesky" | custom-call | tf_op jit(solution)/shard_map/jit(cholesky)/cholesky | solution.py:58
  520.0 9.8 %custom-call.75 = f32[1,128,128]{1,2,0:T(8,128)S(1)} custom-call(f32[1,128,128]{2,1,0:T(8,128)S(1)} %get-tuple-element.69), custom_call_target="InvertDiagBlocksLowerTriangular" | custom-call | tf_op jit(solution)/shard_map/jit(cholesky)/cholesky | solution.py:58
  533.4 12.2 %cholesky.603 = f32[128,128]{1,0:T(8,128)S(1)} custom-call(f32[128,128]{1,0:T(8,128)S(1)} %cholesky.687), custom_call_target="Cholesky" | custom-call | tf_op jit(solution)/shard_map/jit(cholesky)/cholesky | solution.py:58
  546.2 9.8 %custom-call.76 = f32[1,128,128]{1,2,0:T(8,128)S(1)} custom-call(f32[1,128,128]{2,1,0:T(8,128)S(1)} %get-tuple-element.66), custom_call_target="InvertDiagBlocksLowerTriangular" | custom-call | tf_op jit(solution)/shard_map/jit(cholesky)/cholesky | solution.py:58
  559.2 11.7 %cholesky.623 = f32[128,128]{1,0:T(8,128)S(1)} custom-call(f32[128,128]{1,0:T(8,128)S(1)} %cholesky.692), custom_call_target="Cholesky" | custom-call | tf_op jit(solution)/shard_map/jit(cholesky)/cholesky | solution.py:58
  571.6 9.8 %custom-call.77 = f32[1,128,128]{1,2,0:T(8,128)S(1)} custom-call(f32[1,128,128]{2,1,0:T(8,128)S(1)} %get-tuple-element.63), custom_call_target="InvertDiagBlocksLowerTriangular" | custom-call | tf_op jit(solution)/shard_map/jit(cholesky)/cholesky | solution.py:58
  584.0 11.9 %cholesky.641 = f32[128,128]{1,0:T(8,128)S(1)} custom-call(f32[128,128]{1,0:T(8,128)S(1)} %convolution_subtract_fusion.12), custom_call_target="Cholesky" | custom-call | tf_op jit(solution)/shard_map/jit(cholesky)/cholesky | solution.py:58
  607.3 5.4 select_select_fusion
  612.7 30.7 %while.1 = (s32[]{:T(128)}, f32[1152,1152]{1,0:T(8,128)}, s32[9,2]{0,1:T(2,128)S(1)}, f32[9,128,128]{2,1,0:T(8,128)}, s32[]{:T(128)}) while((s32[]{:T(128)}, f32[1152,1152]{1,0:T(8,128)}, s32[9,2]{0,1:T(2,128)S(1)}, f32[9,128,128]{2,1,0:T(8,128)}, s32[]{:T(128)}) %tuple.73), condition=%wide.while_cond, body=%wide.while_body.sunk | while | flops 2 | bytes 132205 | solution.py:59
  643.4 89.2 %custom-call.78 = f32[9,128,128]{1,2,0:T(8,128)S(1)} custom-call(f32[9,128,128]{2,1,0:T(8,128)} %get-tuple-element.9), custom_call_target="InvertDiagBlocksLowerTriangular" | custom-call | tf_op jit(solution)/shard_map/triangular_solve | solution.py:59
  755.4 3.6 convolution_subtract_fusion.3
  760.4 3.7 convolution_subtract_fusion.9
  765.5 7.6 convert_reduce_fusion
  773.2 19.1 %subtract_bitcast_fusion = f32[1,4608,576]{1,2,0:T(8,128)} fusion(bf16[2048,4608]{1,0:T(8,128)(2,1)} %bitcast.4, f32[576]{0:T(1024)S(1)} %dynamic_slice.7, f32[4608]{0:T(1024)S(1)} %broadcast_divide_fusion, f32[]{:T(128)S(6)} %convert_element_type.11, s32[]{:T(128)S(6)} %select_n.38), kind=kOutput, calls=%fused_computation.4 | convolution fusion | flops 10879598592 | bytes 32133384 | tf_op jit(solution)/shard_map/dot_general | solution.py:43
  (115 shorter events, 109.8 us)
Async XLA Ops:
  7.2 347.9 %all-reduce.4.cloned.1.call-start = ((), (), s32[]{:S(2)}) async-start(), calls=%async_computation.2 | async-start | bytes 11796480 | tf_op jit(solution)/shard_map/psum | solution.py:9
  9.9 3.4 copy-start
  13.3 0.7 copy-start.5
  13.3 12.7 %copy-start.4 = (bf16[128,4608]{1,0:T(8,128)(2,1)S(1)}, bf16[128,4608]{1,0:T(8,128)(2,1)}, u32[]{:S(2)}) copy-start(bf16[128,4608]{1,0:T(8,128)(2,1)} %param.3) | copy-start | bytes 3538948
  15.3 32.2 %all-to-all-start.1 = ((s32[128,1,1]{2,1,0:T(1,128)}), s32[128,1,1]{2,1,0:T(1,128)}, u32[]{:S(2)}, u32[]{:S(2)}) async-start(s32[128,1,1]{2,1,0:T(1,128)} %broadcast_in_dim.30), calls=%async_computation.1 | async-start | bytes 131072 | tf_op jit(solution)/shard_map/all_to_all | solution.py:34
  54.4 711.1 %all-to-all-start = ((bf16[128,16,4608]{2,1,0:T(8,128)(2,1)}), bf16[128,16,4608]{2,1,0:T(8,128)(2,1)}, u32[]{:S(2)}, u32[]{:S(2)}) async-start(bf16[128,16,4608]{2,1,0:T(8,128)(2,1)} %bitcast.136), calls=%async_computation | async-start | bytes 37748736 | tf_op jit(solution)/shard_map/all_to_all | solution.py:27
  361.1 7.2 copy-start.3
  372.7 2.3 copy-start.2
  607.3 125.4 %copy-start.1 = (f32[1,576,1152]{1,2,0:T(8,128)S(1)}, f32[1,576,1152]{1,2,0:T(8,128)}, u32[]{:S(2)}) copy-start(f32[1,576,1152]{1,2,0:T(8,128)} %copy-done) | copy-start | bytes 7962628
Sparse Core Ops, SparseCore 0:
  13.5 341.5 all-reduce.3
where the time goes:
time: 801 us; the launch traced here: 800 us
  other arithmetic  313 us (39%)
  waiting for transfers between devices  288 us (36%)
  matrix products  80.1 us (10%)
  local copies, waits for them, and re-layouts  76.1 us (10%)
  between operations  21 us (3%)
  starting transfers between devices  20.7 us (3%)
    psum x1, waiting for transfers between devices, from_root(): return lax.psum(jnp.where(mine, value, jnp.zeros_like(value)), axis)  288 us
    another operation x34, other arithmetic, body(): lower_factor = jnp.linalg.cholesky(leading)  196 us
    another operation x3, other arithmetic, body(): lax.linalg.triangular_solve(lower_factor, previous[0], left_side=False, l...  94.6 us
    another operation x17, matrix products, body(): lax.linalg.triangular_solve(lower_factor, previous[0], left_side=False, l...  32.8 us
    another operation x27, local copies, waits for them, and re-layouts  30.7 us
    another operation x16, matrix products, body(): lower_factor = jnp.linalg.cholesky(leading)  28.2 us
    scatter x1, local copies, waits for them, and re-layouts, body(): jnp.zeros((classes, capacity, width), jnp.bfloat16).at[label_col, ranks]  21.4 us
    dot_general x1, matrix products, body(): lax.dot_general(flattened, tile_cols, (((0,), (0,)), ((), ())), preferred...  19.1 us
  transfers between devices with their start and end apart: 3, of which 1 were waited for; matrix products, arithmetic and copies ran while one was open for 54% of the time, Pallas kernels for 0%

commit v1 on v0

v1 whole, which is shorter than its diff:
```python
import functools

import jax
import jax.numpy as jnp
from jax import lax
from jax.experimental import pallas as pl
from jax.experimental.pallas import tpu as pltpu
from jax.sharding import PartitionSpec as P

MESH = pl.DeviceIdType.MESH
HI = lax.Precision.HIGHEST
D = 4608
CAP = 16
CLS = 16
FEAT = 8
PW = 2560
QW = D - PW
SLOT = CAP * CLS
HALF = SLOT // 2
TILE = D // FEAT
WIN = 640
PANEL = 1152
OWN = 576
ROWS = 1792
NB = 128
COLS = 384
NPAN = 3
PIECE = (144, 96, 48)
LPW = 128
LHS = TILE + 16


def dot_t(a, b):
    return lax.dot_general(a, b, (((1,), (1,)), ((), ())), precision=HI, preferred_element_type=jnp.float32)


def dot_ta(a, b):
    return lax.dot_general(a, b, (((0,), (0,)), ((), ())), precision=HI, preferred_element_type=jnp.float32)


def diag_inverse(W, r0, SA, SM):
    SA[...] = W[pl.ds(r0, NB), pl.ds(r0, NB)]
    row = lax.broadcasted_iota(jnp.int32, (NB, NB), 0)
    col = lax.broadcasted_iota(jnp.int32, (NB, NB), 1)
    SM[...] = jnp.where(row == col, 1.0, 0.0).astype(jnp.float32)
    sub = lax.broadcasted_iota(jnp.int32, (8, NB), 0)
    for g in range(NB // 8):
        lo = 8 * g
        pa = SA[lo : lo + 8, :]
        pm = SM[lo : lo + 8, :]
        cols = [jnp.broadcast_to(pa[:, lo + t : lo + t + 1], (8, NB)) for t in range(8)]
        scale = jnp.zeros((8, NB), jnp.float32)
        for t in range(8):
            piv = jnp.broadcast_to(cols[t][t : t + 1, :], (8, NB))
            m = jnp.where(sub > t, cols[t] * (1.0 / piv), 0.0)
            scale = jnp.where(sub == t, piv, scale)
            for u in range(t + 1, 8):
                cols[u] = cols[u] - m * jnp.broadcast_to(cols[u][t : t + 1, :], (8, NB))
            pa = pa - m * jnp.broadcast_to(pa[t : t + 1, :], (8, NB))
            pm = pm - m * jnp.broadcast_to(pm[t : t + 1, :], (8, NB))
        s = lax.rsqrt(scale)
        y = pa * s
        z = pm * s
        SM[lo : lo + 8, :] = z
        if g < NB // 8 - 1:
            n0 = lo + 8
            upd = dot_ta(y, jnp.concatenate([y, z], axis=1))
            SA[n0:, :] = SA[n0:, :] - upd[n0:, :NB]
            SM[n0:, :] = SM[n0:, :] - upd[n0:, NB:]


def chol_step(W, k, SA, SM, hook):
    r0 = pl.multiple_of(k * NB, NB)
    b = lax.rem(k, 3)
    s = k // 3
    for st in (1, 2):

        @pl.when((b == 0) & (s == st))
        def _():
            c0 = 384 * st

            def body(i, _):
                r = pl.multiple_of(c0 + i * 128, 128)
                acc = W[pl.ds(r, 128), c0 : c0 + 384]
                for q in range(st):
                    acc = acc - dot_t(
                        W[pl.ds(r, 128), 384 * q : 384 * q + 384], W[c0 : c0 + 384, 384 * q : 384 * q + 384]
                    )
                W[pl.ds(r, 128), c0 : c0 + 384] = acc
                return 0

            lax.fori_loop(0, (ROWS - c0) // 128, body, 0)

    diag_inverse(W, r0, SA, SM)
    hook(0)

    def tb(i, _):
        r = pl.multiple_of(i * 256, 256)
        W[pl.ds(r, 256), pl.ds(r0, NB)] = dot_t(W[pl.ds(r, 256), pl.ds(r0, NB)], SM[...])
        return 0

    lax.fori_loop((k + 1) // 2, ROWS // 256, tb, 0)
    for bb in (0, 1):

        @pl.when(b == bb)
        def _():
            n = 256 - 128 * bb

            def ub(i, _):
                r = pl.multiple_of(i * 256, 256)
                c1 = pl.multiple_of(r0 + NB, NB)
                W[pl.ds(r, 256), pl.ds(c1, n)] = W[pl.ds(r, 256), pl.ds(c1, n)] - dot_t(
                    W[pl.ds(r, 256), pl.ds(r0, NB)], W[pl.ds(c1, n), pl.ds(r0, NB)]
                )
                return 0

            lax.fori_loop((k + 1) // 2, ROWS // 256, ub, 0)


def kernel(
    stp, stq, cst, prev,
    gram, panel, ssum, tsum, cnt,
    GP, GQ, W, XT, TT, LT, SA, SM, C1, C2,
    p1r, p1s, lr, ls, lxs, lxr, lzs, lzr, xs, xr, zs, zr, ps, pr, cr, cs, own_sem,
):
    c = lax.axis_index("cls")
    f = lax.axis_index("feat")
    x = lax.rem(f, 4)
    zoff = f - x
    zmate = 4 - zoff
    mate = x + zmate
    zhi = lax.rem(c // 2, 2)

    def at_x(d, z):
        return z + lax.rem(x + d, 4)

    right, left, far = at_x(1, zoff), at_x(3, zoff), at_x(2, zoff)

    bar = pltpu.get_barrier_semaphore()

    def sig(cc, ff):
        pl.semaphore_signal(bar, inc=1, device_id=(cc, ff), device_id_type=MESH)

    def sig_cls(cc, _):
        @pl.when(cc != c)
        def _():
            sig(cc, f)

        sig(cc, mate)
        return 0

    lax.fori_loop(0, CLS, sig_cls, 0)
    for d in (1, 2, 3):
        sig(c, at_x(d, zoff))
        sig(c, at_x(d, zmate))
    pl.semaphore_wait(bar, 37)

    def put(src, dst, dev, ssem, rsem):
        pltpu.make_async_remote_copy(
            src_ref=src, dst_ref=dst, send_sem=ssem, recv_sem=rsem, device_id=dev, device_id_type=MESH
        ).start()

    def wait(ref, sem):
        pltpu.make_async_copy(ref, ref, sem).wait()

    def put_same(ref, ff, ssem, rsem):
        put(ref, ref, (c, ff), ssem, rsem)

    def piece(j, i, lo=0, hi=COLS):
        r = pl.multiple_of(COLS * j + PIECE[j] * i, 8)
        return W.at[pl.ds(r, PIECE[j]), COLS * j + lo : COLS * j + hi]

    for src in (0, 1):

        @pl.when(f == src)
        def _():
            for j in range(NPAN):
                for i in range(FEAT):
                    r = COLS * j + PIECE[j] * i
                    if r // OWN != src:
                        continue
                    r = r - OWN * src
                    ref = prev.at[r : r + PIECE[j], COLS * j : COLS * (j + 1)]
                    if i == src:
                        pltpu.make_async_copy(ref, piece(j, i), lr.at[j]).start()
                    else:
                        put(ref, piece(j, i), (c, i), ls.at[j], lr.at[j])

    own_copy = pltpu.make_async_copy(prev, W.at[PANEL : PANEL + OWN, :], own_sem)
    own_copy.start()

    def route(cc, _):
        same = lax.rem(cc // 2, 2) == zhi
        g = jnp.where(same, f, mate)
        r = pl.multiple_of(CAP * c, CAP)
        dq = GQ.at[g, pl.ds(r, CAP), :]

        @pl.when(cc == c)
        def _():
            pltpu.make_async_copy(stq.at[cc], dq, p1r.at[0]).start()
            pltpu.make_async_copy(cst.at[cc], C1.at[c], cr.at[0]).start()

        @pl.when(cc != c)
        def _():
            put(stq.at[cc], dq, (cc, g), p1s.at[0], p1r.at[0])
            put(cst.at[cc], C1.at[c], (cc, f), cs.at[0], cr.at[0])

        return 0

    lax.fori_loop(0, CLS, route, 0)

    def route_p(cc, _):
        same = lax.rem(cc // 2, 2) == zhi
        g = jnp.where(same, f, mate)
        r = pl.multiple_of(CAP * c, CAP)
        dp = GP.at[g, pl.ds(r, CAP), :]

        @pl.when(cc == c)
        def _():
            pltpu.make_async_copy(stp.at[cc], dp, p1r.at[1]).start()

        @pl.when(cc != c)
        def _():
            put(stp.at[cc], dp, (cc, g), p1s.at[1], p1r.at[1])

        return 0

    lax.fori_loop(0, CLS, route_p, 0)

    def zero(i, _):
        gram[:, pl.ds(pl.multiple_of(512 * i, 512), 512)] = jnp.zeros((TILE, 512), jnp.float32)
        return 0

    lax.fori_loop(0, D // 512, zero, 0)
    ssum[...] = jnp.zeros_like(ssum)
    tsum[...] = jnp.zeros_like(tsum)
    LT[TILE:, :] = jnp.ones((LHS - TILE, SLOT), jnp.bfloat16)
    W[PANEL + OWN :, :] = jnp.zeros((ROWS - PANEL - OWN, PANEL), jnp.float32)

    along_x = ((0, right), (1, left), (2, far))
    from_x = ((0, 3), (1, 1), (2, 2))

    def lead_a(j):
        wait(piece(j, f), lr.at[j])
        put_same(piece(j, f, 0, LPW), mate, lzs.at[j, 0], lzr.at[j, 0])
        for d, ff in along_x:
            put_same(piece(j, f), ff, lxs.at[j, d], lxr.at[j, d])
        put_same(piece(j, f, LPW), mate, lzs.at[j, 1], lzr.at[j, 1])

    def lead_b(j):
        wait(piece(j, mate, 0, LPW), lzr.at[j, 0])
        for d, ff in along_x:
            put_same(piece(j, mate, 0, LPW), ff, lxs.at[j, 3 + d], lxr.at[j, 3 + d])

    def lead_c(j):
        for d, off in from_x:
            wait(piece(j, at_x(off, zoff)), lxr.at[j, d])
            put_same(piece(j, at_x(off, zoff), LPW), mate, lzs.at[j, 2 + d], lzr.at[j, 2 + d])

    def lead_d(j):
        wait(piece(j, mate, LPW), lzr.at[j, 1])
        for d, off in from_x:
            wait(piece(j, at_x(off, zmate), 0, LPW), lxr.at[j, 3 + d])
            wait(piece(j, at_x(off, zmate), LPW), lzr.at[j, 2 + d])
        wait(piece(j, f, 0, LPW), lzs.at[j, 0])
        wait(piece(j, f, LPW), lzs.at[j, 1])
        for d in range(3):
            wait(piece(j, f), lxs.at[j, d])
            wait(piece(j, mate, 0, LPW), lxs.at[j, 3 + d])
            wait(piece(j, f, LPW), lzs.at[j, 2 + d])

    def block(st, xoff, h):
        ref = GQ if st == 0 else GP
        slot = at_x(xoff, zmate if st == 2 else zoff)
        return ref.at[slot, HALF * h : HALF * (h + 1), :]

    def send_own(st):
        for h in (0, 1):
            put_same(block(st, 0, h), right, xs.at[st, 0, h], xr.at[st, 0, h])
            put_same(block(st, 0, 1 - h), left, xs.at[st, 1, 1 - h], xr.at[st, 1, 1 - h])

    def to_mate(d, h):
        b = GQ.at[at_x(d, zoff), HALF * h : HALF * (h + 1), :]
        put_same(b, mate, zs.at[d, h], zr.at[d, h])

    def start_q():
        wait(GQ.at[f], p1r.at[0])
        to_mate(0, 0)
        to_mate(0, 1)
        send_own(0)

    def start_p():
        wait(GP.at[f], p1r.at[1])
        put_same(GP.at[f], mate, ps, pr)
        send_own(1)

    def start_mate_p():
        wait(GP.at[mate], pr)
        send_own(2)

    def forward(st, last):
        if not last:
            wait(block(st, 3, 0), xr.at[st, 0, 0])
            put_same(block(st, 3, 0), right, xs.at[st, 2, 0], xr.at[st, 2, 0])
            wait(block(st, 1, 1), xr.at[st, 1, 1])
            put_same(block(st, 1, 1), left, xs.at[st, 2, 1], xr.at[st, 2, 1])
            if st == 0:
                to_mate(3, 0)
                to_mate(1, 1)
        else:
            wait(block(st, 3, 1), xr.at[st, 0, 1])
            wait(block(st, 1, 0), xr.at[st, 1, 0])
            if st == 0:
                to_mate(3, 1)
                to_mate(1, 0)

    def far_in(st):
        for h in (0, 1):
            wait(block(st, 2, h), xr.at[st, 2, h])
            if st == 0:
                to_mate(2, h)

    def mate_q(d):
        for h in (0, 1):
            wait(GQ.at[at_x(d, zmate), HALF * h : HALF * (h + 1), :], zr.at[d, h])

    def count():
        wait(C1, cr.at[0])
        C2[f] = jnp.sum(C1[...], axis=0)
        for d in (1, 2, 3):
            put_same(C2.at[f], at_x(d, zoff), cs.at[1], cr.at[1])
        for d in (0, 1, 2, 3):
            put_same(C2.at[f], at_x(d, zmate), cs.at[1], cr.at[1])

    base = (9 * f) // 2
    half_tile = 64 * lax.rem(f, 2)

    def gram_slot(s):
        for i in range(WIN // 128):
            j = base + i
            dst = slice(128 * i, 128 * (i + 1))

            @pl.when(j < PW // 128)
            def _():
                XT[:, dst] = GP[s, :, pl.ds(pl.multiple_of(128 * j, 128), 128)]

            @pl.when(j >= PW // 128)
            def _():
                XT[:, dst] = GQ[s, :, pl.ds(pl.multiple_of(128 * (j - PW // 128), 128), 128)]

        TT[...] = XT[...].T
        LT[:TILE, :] = TT[pl.ds(pl.multiple_of(half_tile, 64), TILE), :]
        tsum[...] += jnp.dot(LT[:TILE, :], jnp.ones((SLOT, 128), jnp.bfloat16), preferred_element_type=jnp.float32)
        for ref, n, r0 in ((GP, PW, 0), (GQ, QW, PW)):

            def chunk(i, _):
                q = pl.multiple_of(512 * i, 512)
                r = pl.ds(pl.multiple_of(r0 + q, 512), 512)
                acc = jnp.dot(LT[...], ref[s, :, pl.ds(q, 512)], preferred_element_type=jnp.float32)
                gram[:, r] += acc[:TILE]
                ssum[:, r] += acc[TILE:]
                return 0

            lax.fori_loop(0, n // 512, chunk, 0)

    lead_a(0)
    start_q()
    lead_b(0)
    lead_c(0)
    start_p()
    lead_d(0)
    own_copy.wait()

    events = {
        0: [lambda: lead_a(1), lambda: lead_a(2)],
        1: [lambda: lead_b(1), lambda: lead_b(2), start_mate_p],
        2: [lambda: lead_c(1), lambda: lead_c(2), count],
        3: [lambda: forward(0, False)],
        4: [lambda: lead_d(1), lambda: forward(0, True)],
        5: [lambda: lead_d(2), lambda: forward(1, False)],
        6: [lambda: far_in(0)],
        8: [lambda: mate_q(0)],
        9: [lambda: forward(2, False)],
        13: [lambda: forward(1, True)],
    }

    def hooks(k, place):
        for at, evs in events.items():
            if at % 2 == place:

                @pl.when(k == at // 2)
                def _():
                    for ev in evs:
                        ev()

    def step(k, _):
        chol_step(W, k, SA, SM, functools.partial(hooks, k))
        hooks(k, 1)

        @pl.when((k == 1) | (k == 4) | (k >= 7))
        def _():
            gram_slot(jnp.where(k == 1, f, jnp.where(k == 4, mate, jnp.where(k == 7, right, left))))

        return 0

    lax.fori_loop(0, PANEL // NB, step, 0)
    panel[...] = W[PANEL : PANEL + OWN, :]

    far_in(1)
    gram_slot(far)
    forward(2, True)
    mate_q(1)
    gram_slot(at_x(1, zmate))
    mate_q(3)
    gram_slot(at_x(3, zmate))
    far_in(2)
    mate_q(2)
    gram_slot(at_x(2, zmate))

    wait(C2.at[0:7], cr.at[1])
    cnt[...] = jnp.sum(C2[...], axis=0)

    for src, rows in ((0, (432, 96, 0)), (1, (576, 576, 336))):

        @pl.when(f == src)
        def _():
            for j in range(NPAN):
                if rows[j]:
                    wait(prev.at[0 : rows[j], 0:COLS], ls.at[j])

    wait(stq.at[0:15], p1s.at[0])
    wait(stp.at[0:15], p1s.at[1])
    wait(cst.at[0:15], cs.at[0])
    wait(C2.at[0:7], cs.at[1])
    wait(GP.at[f], ps)
    for st in range(3):
        for d in range(3):
            for h in (0, 1):
                wait(block(st, 0, h), xs.at[st, d, h])
    for d in range(4):
        for h in (0, 1):
            wait(GQ.at[f, HALF * h : HALF * (h + 1), :], zs.at[d, h])


def exchange(stp, stq, cst, prev):
    dma = pltpu.SemaphoreType.DMA
    any_space = pl.BlockSpec(memory_space=pl.ANY)
    vmem = pl.BlockSpec(memory_space=pltpu.VMEM)
    return pl.pallas_call(
        kernel,
        out_shape=(
            jax.ShapeDtypeStruct((TILE, D), jnp.float32),
            jax.ShapeDtypeStruct((OWN, PANEL), jnp.float32),
            jax.ShapeDtypeStruct((LHS - TILE, D), jnp.float32),
            jax.ShapeDtypeStruct((TILE, 128), jnp.float32),
            jax.ShapeDtypeStruct((8, 128), jnp.float32),
        ),
        in_specs=[any_space] * 4,
        out_specs=(vmem,) * 5,
        scratch_shapes=[
            pltpu.VMEM((FEAT, SLOT, PW), jnp.bfloat16),
            pltpu.VMEM((FEAT, SLOT, QW), jnp.bfloat16),
            pltpu.VMEM((ROWS, PANEL), jnp.float32),
            pltpu.VMEM((SLOT, WIN), jnp.bfloat16),
            pltpu.VMEM((WIN, SLOT), jnp.bfloat16),
            pltpu.VMEM((LHS, SLOT), jnp.bfloat16),
            pltpu.VMEM((NB, NB), jnp.float32),
            pltpu.VMEM((NB, NB), jnp.float32),
            pltpu.VMEM((CLS, 8, 128), jnp.float32),
            pltpu.VMEM((FEAT, 8, 128), jnp.float32),
            dma((2,)),
            dma((2,)),
            dma((NPAN,)),
            dma((NPAN,)),
            dma((NPAN, 6)),
            dma((NPAN, 6)),
            dma((NPAN, 5)),
            dma((NPAN, 5)),
            dma((3, 3, 2)),
            dma((3, 3, 2)),
            dma((4, 2)),
            dma((4, 2)),
            dma(()),
            dma(()),
            dma((2,)),
            dma((2,)),
            dma(()),
        ],
        compiler_params=pltpu.CompilerParams(
            collective_id=0, has_side_effects=True, vmem_limit_bytes=60 * 2**20
        ),
        cost_estimate=pl.CostEstimate(flops=2 * 2048 * 4608 * 640, bytes_accessed=40 * 2**20, transcendentals=0),
    )(stp, stq, cst, prev)


def body(embeddings, labels, previous):
    rows = embeddings.shape[0]
    label = labels[:, 0]
    onehot = (label[:, None] == jnp.arange(CLS, dtype=jnp.int32)[None, :]).astype(jnp.float32)
    before = (jnp.arange(rows)[:, None] > jnp.arange(rows)[None, :]).astype(jnp.float32)
    rank = jnp.sum(jnp.dot(before, onehot) * onehot, axis=1).astype(jnp.int32)
    place = label * CAP + rank
    pick = (jnp.arange(CLS * CAP, dtype=jnp.int32)[:, None] == place[None, :]).astype(jnp.bfloat16)
    stp = jnp.dot(pick, embeddings[:, :PW]).reshape(CLS, CAP, PW)
    stq = jnp.dot(pick, embeddings[:, PW:]).reshape(CLS, CAP, QW)
    counts = jnp.sum(onehot, axis=0)
    cst = jnp.broadcast_to(counts[:, None, None], (CLS, 8, 128))
    gram, panel, ssum, tsum, cnt = exchange(stp, stq, cst, previous[0])
    total = cnt[0, 0]
    class_cov = (gram / total - (tsum[:, :1] / total) * (ssum[:1, :] / total)).T
    return class_cov[None], panel[None]


def solution(mesh):
    return jax.shard_map(
        body,
        mesh=mesh,
        in_specs=(P(("cls", "feat"), None), P(("cls", "feat"), None), P("cls", "feat", None)),
        out_specs=(P("cls", None, "feat"), P("cls", "feat", None)),
        check_vma=False,
    )
```

time: 801 us -> 273 us (0.34)
  the two profiles are of different devices: /device:TPU:119 before, /device:TPU:0 now
where the time goes in v1:
time: 273 us; the launch traced here: 272 us
  Pallas kernels  247 us (90%)
  other arithmetic  15.5 us (6%)
  matrix products  5.95 us (2%)
  local copies, waits for them, and re-layouts  3.41 us (1%)
    pallas_call x1, Pallas kernels, exchange(): pl.pallas_call(kernel, out_shape=(jax.ShapeDtypeStruct((TILE, D), jnp.flo...  247 us
    broadcast_in_dim x1, other arithmetic, body(): return (class_cov[None], panel[None])  10.6 us

profile of v1, /device:TPU:0, one launch (start us, length us, event | category | flops | bytes accessed | tf_op | source)
XLA Modules:
  0.0 272.4 jit_solution(7671512118538726329)
XLA Ops:
  0.6 0.8 convert_reduce_fusion
  1.4 0.9 fusion
  2.3 0.7 convert_add_fusion
  3.0 0.7 broadcast_in_dim.6.cst
  3.7 2.4 fusion.3
  6.1 2.6 fusion.1
  8.7 246.9 %shard_map.50 = (f32[576,4608]{1,0:T(8,128)}, f32[576,1152]{1,0:T(8,128)}, f32[16,4608]{1,0:T(8,128)}, f32[576,128]{1,0:T(8,128)}, f32[8,128]{1,0:T(8,128)}) custom-call(bf16[16,16,2560]{2,1,0:T(8,128)(2,1)} %bitcast.12, bf16[16,16,2048]{2,1,0:T(8,128)(2,1)} %bitcast.13, f32[16,8,128]{2,1,0:T(8,128)} %broadcast_in_dim.6.cst, f32[576,1152]{1,0:T(8,128)} %bitcast.14), custom_call_target="tpu_custom_call" | custom-call | flops 12079595520 | bytes 41943040 | tf_op jit(solution)/shard_map/pallas_call | solution.py:449
  255.6 1.2 slice.17
  256.8 1.8 fusion.5
  258.6 1.6 divide_reduce_fusion
  260.2 0.0 copy-start
  260.2 10.6 %subtract_bitcast_fusion = f32[1,4608,576]{1,2,0:T(8,128)} fusion(f32[576,4608]{1,0:T(8,128)} %get-tuple-element.7, f32[4608]{0:T(1024)S(1)} %divide_reduce_fusion, f32[576]{0:T(1024)S(1)} %fusion.5, f32[]{:T(128)} %bitcast.4), kind=kLoop, calls=%fused_computation | loop fusion | flops 7962624 | bytes 21254404 | tf_op jit(solution)/shard_map/broadcast_in_dim | solution.py:511
  270.8 0.0 copy-done
  270.8 1.5 copy.6
Async XLA Ops:
  260.2 10.6 %copy-start = (f32[576,1152]{1,0:T(8,128)S(1)}, f32[576,1152]{1,0:T(8,128)}, u32[]{:S(2)}) copy-start(f32[576,1152]{1,0:T(8,128)} %get-tuple-element.11) | copy-start | bytes 7962628

commit v2 on v1

--- a/solution.py
+++ b/solution.py
@@ -34,10 +34,6 @@
     return lax.dot_general(a, b, (((1,), (1,)), ((), ())), precision=HI, preferred_element_type=jnp.float32)
 
 
-def dot_ta(a, b):
-    return lax.dot_general(a, b, (((0,), (0,)), ((), ())), precision=HI, preferred_element_type=jnp.float32)
-
-
 def diag_inverse(W, r0, SA, SM):
     SA[...] = W[pl.ds(r0, NB), pl.ds(r0, NB)]
     row = lax.broadcasted_iota(jnp.int32, (NB, NB), 0)
@@ -50,23 +46,32 @@
         pm = SM[lo : lo + 8, :]
         cols = [jnp.broadcast_to(pa[:, lo + t : lo + t + 1], (8, NB)) for t in range(8)]
         scale = jnp.zeros((8, NB), jnp.float32)
+        invs, rows_a, rows_m, heads = [], [], [], []
         for t in range(8):
-            piv = jnp.broadcast_to(cols[t][t : t + 1, :], (8, NB))
-            m = jnp.where(sub > t, cols[t] * (1.0 / piv), 0.0)
-            scale = jnp.where(sub == t, piv, scale)
+            heads.append([jnp.broadcast_to(cols[u][t : t + 1, :], (8, NB)) for u in range(8)])
+            rows_a.append(jnp.broadcast_to(pa[t : t + 1, :], (8, NB)))
+            rows_m.append(jnp.broadcast_to(pm[t : t + 1, :], (8, NB)))
+            invs.append(1.0 / heads[t][t])
+            m = jnp.where(sub > t, cols[t] * invs[t], 0.0)
+            scale = jnp.where(sub == t, heads[t][t], scale)
             for u in range(t + 1, 8):
-                cols[u] = cols[u] - m * jnp.broadcast_to(cols[u][t : t + 1, :], (8, NB))
-            pa = pa - m * jnp.broadcast_to(pa[t : t + 1, :], (8, NB))
-            pm = pm - m * jnp.broadcast_to(pm[t : t + 1, :], (8, NB))
-        s = lax.rsqrt(scale)
-        y = pa * s
-        z = pm * s
-        SM[lo : lo + 8, :] = z
-        if g < NB // 8 - 1:
-            n0 = lo + 8
-            upd = dot_ta(y, jnp.concatenate([y, z], axis=1))
-            SA[n0:, :] = SA[n0:, :] - upd[n0:, :NB]
-            SM[n0:, :] = SM[n0:, :] - upd[n0:, NB:]
+                cols[u] = cols[u] - m * heads[t][u]
+            pa = pa - m * rows_a[t]
+            pm = pm - m * rows_m[t]
+        SM[lo : lo + 8, :] = pm * lax.rsqrt(scale)
+        for i in range(g + 1, NB // 8):
+            r = slice(8 * i, 8 * i + 8)
+            a = SA[r, :]
+            b = SM[r, :]
+            q = [jnp.broadcast_to(a[:, lo + t : lo + t + 1], (8, NB)) for t in range(8)]
+            for t in range(8):
+                m = q[t] * invs[t]
+                a = a - m * rows_a[t]
+                b = b - m * rows_m[t]
+                for u in range(t + 1, 8):
+                    q[u] = q[u] - m * heads[t][u]
+            SA[r, :] = a
+            SM[r, :] = b
 
 
 def chol_step(W, k, SA, SM, hook):
@@ -118,10 +123,10 @@
 
 
 def kernel(
-    stp, stq, cst, prev,
+    emb, lab, prev,
     gram, panel, ssum, tsum, cnt,
-    GP, GQ, W, XT, TT, LT, SA, SM, C1, C2,
-    p1r, p1s, lr, ls, lxs, lxr, lzs, lzr, xs, xr, zs, zr, ps, pr, cr, cs, own_sem,
+    E, STP, STQ, CST, GP, GQ, W, XT, TT, LT, SA, SM, C1, C2,
+    p1r, p1s, lr, ls, lxs, lxr, lzs, lzr, xs, xr, zs, zr, ps, pr, cr, cs, own_sem, emb_sem,
 ):
     c = lax.axis_index("cls")
     f = lax.axis_index("feat")
@@ -149,6 +154,10 @@
         sig(cc, mate)
         return 0
 
+    emb_copy = pltpu.make_async_copy(emb, E, emb_sem)
+    emb_copy.start()
+    own_copy = pltpu.make_async_copy(prev, W.at[PANEL : PANEL + OWN, :], own_sem)
+    own_copy.start()
     lax.fori_loop(0, CLS, sig_cls, 0)
     for d in (1, 2, 3):
         sig(c, at_x(d, zoff))
@@ -186,8 +195,29 @@
                     else:
                         put(ref, piece(j, i), (c, i), ls.at[j], lr.at[j])
 
-    own_copy = pltpu.make_async_copy(prev, W.at[PANEL : PANEL + OWN, :], own_sem)
-    own_copy.start()
+    n = emb.shape[0]
+    label = lab[...].astype(jnp.float32)
+    onehot = (lax.broadcasted_iota(jnp.int32, (CLS, n), 0).astype(jnp.float32) == label).astype(jnp.float32)
+    t0 = lax.broadcasted_iota(jnp.int32, (n, n), 0)
+    t1 = lax.broadcasted_iota(jnp.int32, (n, n), 1)
+    ahead = jnp.dot(
+        onehot.astype(jnp.bfloat16), (t0 < t1).astype(jnp.float32).astype(jnp.bfloat16), preferred_element_type=jnp.float32
+    )
+    place = label * CAP + jnp.sum(ahead * onehot, axis=0, keepdims=True)
+    pick = (lax.broadcasted_iota(jnp.int32, (SLOT, n), 0).astype(jnp.float32) == place).astype(jnp.float32)
+    pick = pick.astype(jnp.bfloat16)
+    counts = jnp.sum(onehot, axis=1, keepdims=True)
+    for i in range(CLS):
+        CST[i] = jnp.broadcast_to(counts[i : i + 1, :], (8, 128))
+    emb_copy.wait()
+    for ref, w, c0 in ((STQ, QW, PW), (STP, PW, 0)):
+        for i in range(w // 512):
+            cols = slice(512 * i, 512 * (i + 1))
+            chosen = jnp.dot(pick, E[:, c0 + 512 * i : c0 + 512 * (i + 1)], preferred_element_type=jnp.float32)
+            ref[:, cols] = chosen.astype(jnp.bfloat16)
+
+    def rows_of(ref, cc):
+        return ref.at[pl.ds(pl.multiple_of(CAP * cc, CAP), CAP), :]
 
     def route(cc, _):
         same = lax.rem(cc // 2, 2) == zhi
@@ -197,13 +227,13 @@
 
         @pl.when(cc == c)
         def _():
-            pltpu.make_async_copy(stq.at[cc], dq, p1r.at[0]).start()
-            pltpu.make_async_copy(cst.at[cc], C1.at[c], cr.at[0]).start()
+            pltpu.make_async_copy(rows_of(STQ, cc), dq, p1r.at[0]).start()
+            pltpu.make_async_copy(CST.at[cc], C1.at[c], cr.at[0]).start()
 
         @pl.when(cc != c)
         def _():
-            put(stq.at[cc], dq, (cc, g), p1s.at[0], p1r.at[0])
-            put(cst.at[cc], C1.at[c], (cc, f), cs.at[0], cr.at[0])
+            put(rows_of(STQ, cc), dq, (cc, g), p1s.at[0], p1r.at[0])
+            put(CST.at[cc], C1.at[c], (cc, f), cs.at[0], cr.at[0])
 
         return 0
 
@@ -217,15 +247,14 @@
 
         @pl.when(cc == c)
         def _():
-            pltpu.make_async_copy(stp.at[cc], dp, p1r.at[1]).start()
+            pltpu.make_async_copy(rows_of(STP, cc), dp, p1r.at[1]).start()
 
         @pl.when(cc != c)
         def _():
-            put(stp.at[cc], dp, (cc, g), p1s.at[1], p1r.at[1])
+            put(rows_of(STP, cc), dp, (cc, g), p1s.at[1], p1r.at[1])
 
         return 0
 
-    lax.fori_loop(0, CLS, route_p, 0)
 
     def zero(i, _):
         gram[:, pl.ds(pl.multiple_of(512 * i, 512), 512)] = jnp.zeros((TILE, 512), jnp.float32)
@@ -285,6 +314,7 @@
 
     def start_q():
         wait(GQ.at[f], p1r.at[0])
+        lax.fori_loop(0, CLS, route_p, 0)
         to_mate(0, 0)
         to_mate(0, 1)
         send_own(0)
@@ -364,24 +394,25 @@
             lax.fori_loop(0, n // 512, chunk, 0)
 
     lead_a(0)
+    lead_b(0)
     start_q()
-    lead_b(0)
     lead_c(0)
-    start_p()
+    lead_a(1)
+    lead_a(2)
     lead_d(0)
     own_copy.wait()
 
     events = {
-        0: [lambda: lead_a(1), lambda: lead_a(2)],
-        1: [lambda: lead_b(1), lambda: lead_b(2), start_mate_p],
+        0: [start_p],
+        1: [lambda: lead_b(1), lambda: lead_b(2)],
         2: [lambda: lead_c(1), lambda: lead_c(2), count],
         3: [lambda: forward(0, False)],
         4: [lambda: lead_d(1), lambda: forward(0, True)],
-        5: [lambda: lead_d(2), lambda: forward(1, False)],
-        6: [lambda: far_in(0)],
-        8: [lambda: mate_q(0)],
-        9: [lambda: forward(2, False)],
-        13: [lambda: forward(1, True)],
+        5: [lambda: lead_d(2)],
+        8: [lambda: far_in(0)],
+        9: [lambda: mate_q(0), start_mate_p],
+        13: [lambda: forward(1, False)],
+        15: [lambda: forward(1, True)],
     }
 
     def hooks(k, place):
@@ -397,15 +428,16 @@
         chol_step(W, k, SA, SM, functools.partial(hooks, k))
         hooks(k, 1)
 
-        @pl.when((k == 1) | (k == 4) | (k >= 7))
-        def _():
-            gram_slot(jnp.where(k == 1, f, jnp.where(k == 4, mate, jnp.where(k == 7, right, left))))
+        @pl.when((k == 1) | (k == 5) | (k >= 7))
+        def _():
+            gram_slot(jnp.where(k == 1, f, jnp.where(k == 5, mate, jnp.where(k == 7, right, left))))
 
         return 0
 
     lax.fori_loop(0, PANEL // NB, step, 0)
     panel[...] = W[PANEL : PANEL + OWN, :]
 
+    forward(2, False)
     far_in(1)
     gram_slot(far)
     forward(2, True)
@@ -428,9 +460,9 @@
                 if rows[j]:
                     wait(prev.at[0 : rows[j], 0:COLS], ls.at[j])
 
-    wait(stq.at[0:15], p1s.at[0])
-    wait(stp.at[0:15], p1s.at[1])
-    wait(cst.at[0:15], cs.at[0])
+    wait(STQ.at[0 : 15 * CAP, :], p1s.at[0])
+    wait(STP.at[0 : 15 * CAP, :], p1s.at[1])
+    wait(CST.at[0:15], cs.at[0])
     wait(C2.at[0:7], cs.at[1])
     wait(GP.at[f], ps)
     for st in range(3):
@@ -442,7 +474,7 @@
             wait(GQ.at[f, HALF * h : HALF * (h + 1), :], zs.at[d, h])
 
 
-def exchange(stp, stq, cst, prev):
+def exchange(emb, lab, prev):
     dma = pltpu.SemaphoreType.DMA
     any_space = pl.BlockSpec(memory_space=pl.ANY)
     vmem = pl.BlockSpec(memory_space=pltpu.VMEM)
@@ -455,9 +487,13 @@
             jax.ShapeDtypeStruct((TILE, 128), jnp.float32),
             jax.ShapeDtypeStruct((8, 128), jnp.float32),
         ),
-        in_specs=[any_space] * 4,
+        in_specs=[any_space, vmem, any_space],
         out_specs=(vmem,) * 5,
         scratch_shapes=[
+            pltpu.VMEM((128, D), jnp.bfloat16),
+            pltpu.VMEM((SLOT, PW), jnp.bfloat16),
+            pltpu.VMEM((SLOT, QW), jnp.bfloat16),
+            pltpu.VMEM((CLS, 8, 128), jnp.float32),
             pltpu.VMEM((FEAT, SLOT, PW), jnp.bfloat16),
             pltpu.VMEM((FEAT, SLOT, QW), jnp.bfloat16),
             pltpu.VMEM((ROWS, PANEL), jnp.float32),
@@ -485,30 +521,40 @@
             dma((2,)),
             dma((2,)),
             dma(()),
+            dma(()),
         ],
         compiler_params=pltpu.CompilerParams(
             collective_id=0, has_side_effects=True, vmem_limit_bytes=60 * 2**20
         ),
         cost_estimate=pl.CostEstimate(flops=2 * 2048 * 4608 * 640, bytes_accessed=40 * 2**20, transcendentals=0),
-    )(stp, stq, cst, prev)
+    )(emb, lab, prev)
+
+
+def finish_kernel(gram, ssum, tsum, cnt, out):
+    inv = 1.0 / cnt[0:1, 0:1]
+    out[...] = gram[...] * inv - (tsum[:, 0:1] * inv) * (ssum[0:1, :] * inv)
+
+
+def finish(gram, ssum, tsum, cnt):
+    h = 64
+    return pl.pallas_call(
+        finish_kernel,
+        grid=(TILE // h,),
+        out_shape=jax.ShapeDtypeStruct((TILE, D), jnp.float32),
+        in_specs=[
+            pl.BlockSpec((h, D), lambda i: (i, 0)),
+            pl.BlockSpec((LHS - TILE, D), lambda i: (0, 0)),
+            pl.BlockSpec((h, 128), lambda i: (i, 0)),
+            pl.BlockSpec((8, 128), lambda i: (0, 0)),
+        ],
+        out_specs=pl.BlockSpec((h, D), lambda i: (i, 0)),
+        compiler_params=pltpu.CompilerParams(vmem_limit_bytes=60 * 2**20),
+    )(gram, ssum, tsum, cnt)
 
 
 def body(embeddings, labels, previous):
-    rows = embeddings.shape[0]
-    label = labels[:, 0]
-    onehot = (label[:, None] == jnp.arange(CLS, dtype=jnp.int32)[None, :]).astype(jnp.float32)
-    before = (jnp.arange(rows)[:, None] > jnp.arange(rows)[None, :]).astype(jnp.float32)
-    rank = jnp.sum(jnp.dot(before, onehot) * onehot, axis=1).astype(jnp.int32)
-    place = label * CAP + rank
-    pick = (jnp.arange(CLS * CAP, dtype=jnp.int32)[:, None] == place[None, :]).astype(jnp.bfloat16)
-    stp = jnp.dot(pick, embeddings[:, :PW]).reshape(CLS, CAP, PW)
-    stq = jnp.dot(pick, embeddings[:, PW:]).reshape(CLS, CAP, QW)
-    counts = jnp.sum(onehot, axis=0)
-    cst = jnp.broadcast_to(counts[:, None, None], (CLS, 8, 128))
-    gram, panel, ssum, tsum, cnt = exchange(stp, stq, cst, previous[0])
-    total = cnt[0, 0]
-    class_cov = (gram / total - (tsum[:, :1] / total) * (ssum[:1, :] / total)).T
-    return class_cov[None], panel[None]
+    gram, panel, ssum, tsum, cnt = exchange(embeddings, labels.reshape(1, -1), previous[0])
+    return finish(gram, ssum, tsum, cnt).T[None], panel[None]
 
 
 def solution(mesh):

time: 273 us -> 220 us (0.81)
  Pallas kernels: 247 us -> 217 us
  other arithmetic: 15.5 us -> 0 us
  matrix products: 5.95 us -> 0 us
    pallas_call x1, Pallas kernels: 247 us -> 205 us  [exchange(): pl.pallas_call(kernel, out_shape=(jax.ShapeDtypeStruct((TILE, D), jnp.flo...]
    pallas_call x0 -> x1, Pallas kernels: none -> 12.6 us  [finish(): pl.pallas_call(finish_kernel, grid=(TILE // h,), out_shape=jax.ShapeDtype...]
    broadcast_in_dim x1 -> x0, other arithmetic: 10.6 us -> none  [body(): return (class_cov[None], panel[None])]
    dot_general x3 -> x0, matrix products: 5.95 us -> none  [the longest x1 2.63 us: body(): stp = jnp.dot(pick, embeddings[:, :PW]).reshape(CLS, CAP, PW)]
    div x2 -> x0, other arithmetic: 3.4 us -> none  [body(): class_cov = (gram / total - tsum[:, :1] / total * (ssum[:1, :] / total)).T]
where the time goes in v2:
time: 220 us
  Pallas kernels  217 us (99%)
    pallas_call x1, Pallas kernels, exchange(): pl.pallas_call(kernel, out_shape=(jax.ShapeDtypeStruct((TILE, D), jnp.flo...  205 us
    pallas_call x1, Pallas kernels, finish(): pl.pallas_call(finish_kernel, grid=(TILE // h,), out_shape=jax.ShapeDtype...  12.6 us

profile of v2, /device:TPU:0, one launch (start us, length us, event | category | flops | bytes accessed | tf_op | source)
XLA Modules:
  0.0 219.6 jit_solution(4916242178244548522)
XLA Ops:
  0.6 204.8 %shard_map.50 = (f32[576,4608]{1,0:T(8,128)}, f32[576,1152]{1,0:T(8,128)}, f32[16,4608]{1,0:T(8,128)}, f32[576,128]{1,0:T(8,128)}, f32[8,128]{1,0:T(8,128)}) custom-call(bf16[128,4608]{1,0:T(8,128)(2,1)} %emb.1, s32[1,128]{1,0:T(1,128)} %bitcast.9, f32[576,1152]{1,0:T(8,128)} %bitcast.8), custom_call_target="tpu_custom_call" | custom-call | flops 12079595520 | bytes 41943040 | tf_op jit(solution)/shard_map/pallas_call | solution.py:481
  205.4 0.0 copy-start
  205.5 12.6 %shard_map.51 = f32[576,4608]{1,0:T(8,128)} custom-call(f32[576,4608]{1,0:T(8,128)} %get-tuple-element.7.gram, f32[16,4608]{1,0:T(8,128)} %get-tuple-element.8.ssum, f32[576,128]{1,0:T(8,128)} %get-tuple-element.9.tsum, f32[8,128]{1,0:T(8,128)} %get-tuple-element.10.cnt), custom_call_target="tpu_custom_call" | custom-call | tf_op jit(solution)/shard_map/pallas_call | solution.py:540
  218.1 0.0 copy-done
  218.1 1.5 copy.6
Async XLA Ops:
  205.4 12.7 %copy-start = (f32[576,1152]{1,0:T(8,128)S(1)}, f32[576,1152]{1,0:T(8,128)}, u32[]{:S(2)}) copy-start(f32[576,1152]{1,0:T(8,128)} %get-tuple-element.11) | copy-start | bytes 7962628

commit v3 on v2

--- a/solution.py
+++ b/solution.py
@@ -321,12 +321,16 @@
 
     def start_p():
         wait(GP.at[f], p1r.at[1])
-        put_same(GP.at[f], mate, ps, pr)
+        for h in (0, 1):
+            put_same(block(1, 0, h), mate, ps.at[h], pr.at[h])
         send_own(1)
 
     def start_mate_p():
-        wait(GP.at[mate], pr)
-        send_own(2)
+        for h in (0, 1):
+            wait(block(2, 0, h), pr.at[h])
+            put_same(block(2, 0, h), right if h == 0 else left, xs.at[2, h, h], xr.at[2, h, h])
+        for h in (0, 1):
+            put_same(block(2, 0, h), left if h == 0 else right, xs.at[2, 1 - h, h], xr.at[2, 1 - h, h])
 
     def forward(st, last):
         if not last:
@@ -384,14 +388,15 @@
         for ref, n, r0 in ((GP, PW, 0), (GQ, QW, PW)):
 
             def chunk(i, _):
-                q = pl.multiple_of(512 * i, 512)
-                r = pl.ds(pl.multiple_of(r0 + q, 512), 512)
+                q = 512 * i
+                r = pl.ds(r0 + q, 512)
                 acc = jnp.dot(LT[...], ref[s, :, pl.ds(q, 512)], preferred_element_type=jnp.float32)
                 gram[:, r] += acc[:TILE]
                 ssum[:, r] += acc[TILE:]
                 return 0
 
-            lax.fori_loop(0, n // 512, chunk, 0)
+            for i in range(n // 512):
+                chunk(i, 0)
 
     lead_a(0)
     lead_b(0)
@@ -406,13 +411,14 @@
         0: [start_p],
         1: [lambda: lead_b(1), lambda: lead_b(2)],
         2: [lambda: lead_c(1), lambda: lead_c(2), count],
-        3: [lambda: forward(0, False)],
-        4: [lambda: lead_d(1), lambda: forward(0, True)],
-        5: [lambda: lead_d(2)],
+        4: [lambda: lead_d(1), lambda: forward(0, False)],
+        5: [lambda: lead_d(2), lambda: forward(0, True)],
+        7: [start_mate_p],
         8: [lambda: far_in(0)],
-        9: [lambda: mate_q(0), start_mate_p],
-        13: [lambda: forward(1, False)],
-        15: [lambda: forward(1, True)],
+        11: [lambda: mate_q(0)],
+        12: [lambda: forward(1, False)],
+        14: [lambda: forward(1, True)],
+        16: [lambda: forward(2, False)],
     }
 
     def hooks(k, place):
@@ -428,26 +434,37 @@
         chol_step(W, k, SA, SM, functools.partial(hooks, k))
         hooks(k, 1)
 
-        @pl.when((k == 1) | (k == 5) | (k >= 7))
-        def _():
-            gram_slot(jnp.where(k == 1, f, jnp.where(k == 5, mate, jnp.where(k == 7, right, left))))
+        @pl.when((k == 1) | (k == 6) | (k >= 7))
+        def _():
+            gram_slot(jnp.where(k == 1, f, jnp.where(k == 6, mate, jnp.where(k == 7, right, left))))
 
         return 0
 
     lax.fori_loop(0, PANEL // NB, step, 0)
     panel[...] = W[PANEL : PANEL + OWN, :]
 
-    forward(2, False)
     far_in(1)
-    gram_slot(far)
-    forward(2, True)
-    mate_q(1)
-    gram_slot(at_x(1, zmate))
-    mate_q(3)
-    gram_slot(at_x(3, zmate))
-    far_in(2)
-    mate_q(2)
-    gram_slot(at_x(2, zmate))
+
+    def last(n, _):
+        @pl.when(n == 1)
+        def _():
+            forward(2, True)
+            mate_q(1)
+
+        @pl.when(n == 2)
+        def _():
+            mate_q(3)
+
+        @pl.when(n == 3)
+        def _():
+            far_in(2)
+            mate_q(2)
+
+        d = jnp.where(n == 1, 1, jnp.where(n == 2, 3, 2))
+        gram_slot(at_x(d, jnp.where(n == 0, zoff, zmate)))
+        return 0
+
+    lax.fori_loop(0, 4, last, 0)
 
     wait(C2.at[0:7], cr.at[1])
     cnt[...] = jnp.sum(C2[...], axis=0)
@@ -464,7 +481,8 @@
     wait(STP.at[0 : 15 * CAP, :], p1s.at[1])
     wait(CST.at[0:15], cs.at[0])
     wait(C2.at[0:7], cs.at[1])
-    wait(GP.at[f], ps)
+    for h in (0, 1):
+        wait(block(1, 0, h), ps.at[h])
     for st in range(3):
         for d in range(3):
             for h in (0, 1):
@@ -481,11 +499,11 @@
     return pl.pallas_call(
         kernel,
         out_shape=(
-            jax.ShapeDtypeStruct((TILE, D), jnp.float32),
-            jax.ShapeDtypeStruct((OWN, PANEL), jnp.float32),
-            jax.ShapeDtypeStruct((LHS - TILE, D), jnp.float32),
-            jax.ShapeDtypeStruct((TILE, 128), jnp.float32),
-            jax.ShapeDtypeStruct((8, 128), jnp.float32),
+            pltpu.VMEM((TILE, D), jnp.float32),
+            pltpu.VMEM((OWN, PANEL), jnp.float32),
+            pltpu.VMEM((LHS - TILE, D), jnp.float32),
+            pltpu.VMEM((TILE, 128), jnp.float32),
+            pltpu.VMEM((8, 128), jnp.float32),
         ),
         in_specs=[any_space, vmem, any_space],
         out_specs=(vmem,) * 5,
@@ -516,45 +534,45 @@
             dma((3, 3, 2)),
             dma((4, 2)),
             dma((4, 2)),
-            dma(()),
-            dma(()),
+            dma((2,)),
+            dma((2,)),
             dma((2,)),
             dma((2,)),
             dma(()),
             dma(()),
         ],
         compiler_params=pltpu.CompilerParams(
-            collective_id=0, has_side_effects=True, vmem_limit_bytes=60 * 2**20
+            collective_id=0, has_side_effects=True, vmem_limit_bytes=44 * 2**20
         ),
         cost_estimate=pl.CostEstimate(flops=2 * 2048 * 4608 * 640, bytes_accessed=40 * 2**20, transcendentals=0),
     )(emb, lab, prev)
 
 
-def finish_kernel(gram, ssum, tsum, cnt, out):
+def finish_kernel(gram, panel, ssum, tsum, cnt, out, out_panel):
     inv = 1.0 / cnt[0:1, 0:1]
-    out[...] = gram[...] * inv - (tsum[:, 0:1] * inv) * (ssum[0:1, :] * inv)
-
-
-def finish(gram, ssum, tsum, cnt):
-    h = 64
+    r = pl.ds(pl.multiple_of(64 * pl.program_id(0), 64), 64)
+    out[...] = gram[r, :] * inv - (tsum[r, 0:1] * inv) * (ssum[0:1, :] * inv)
+    out_panel[...] = panel[r, :]
+
+
+def finish(gram, panel, ssum, tsum, cnt):
     return pl.pallas_call(
         finish_kernel,
-        grid=(TILE // h,),
-        out_shape=jax.ShapeDtypeStruct((TILE, D), jnp.float32),
-        in_specs=[
-            pl.BlockSpec((h, D), lambda i: (i, 0)),
-            pl.BlockSpec((LHS - TILE, D), lambda i: (0, 0)),
-            pl.BlockSpec((h, 128), lambda i: (i, 0)),
-            pl.BlockSpec((8, 128), lambda i: (0, 0)),
-        ],
-        out_specs=pl.BlockSpec((h, D), lambda i: (i, 0)),
-        compiler_params=pltpu.CompilerParams(vmem_limit_bytes=60 * 2**20),
-    )(gram, ssum, tsum, cnt)
+        grid=(TILE // 64,),
+        out_shape=(
+            jax.ShapeDtypeStruct((TILE, D), jnp.float32),
+            jax.ShapeDtypeStruct((OWN, PANEL), jnp.float32),
+        ),
+        in_specs=[pl.BlockSpec(memory_space=pltpu.VMEM)] * 5,
+        out_specs=(pl.BlockSpec((64, D), lambda i: (i, 0)), pl.BlockSpec((64, PANEL), lambda i: (i, 0))),
+        compiler_params=pltpu.CompilerParams(vmem_limit_bytes=16 * 2**20),
+    )(gram, panel, ssum, tsum, cnt)
 
 
 def body(embeddings, labels, previous):
     gram, panel, ssum, tsum, cnt = exchange(embeddings, labels.reshape(1, -1), previous[0])
-    return finish(gram, ssum, tsum, cnt).T[None], panel[None]
+    tile, panel = finish(gram, panel, ssum, tsum, cnt)
+    return tile.T[None], panel[None]
 
 
 def solution(mesh):

time: 220 us -> 199 us (0.905)
  Pallas kernels: 217 us -> 198 us
    pallas_call x2, Pallas kernels: 217 us -> 198 us  [the longest x1 191 us: exchange(): pl.pallas_call(kernel, out_shape=(pltpu.VMEM((TILE, D), jnp.float32), plt...]
where the time goes in v3:
time: 199 us; the launch traced here: 198 us
  Pallas kernels  198 us (99%)
    pallas_call x1, Pallas kernels, exchange(): pl.pallas_call(kernel, out_shape=(pltpu.VMEM((TILE, D), jnp.float32), plt...  191 us
    pallas_call x1, Pallas kernels, finish(): pl.pallas_call(finish_kernel, grid=(TILE // 64,), out_shape=(jax.ShapeDty...  6.66 us

profile of v3, /device:TPU:0, one launch (start us, length us, event | category | flops | bytes accessed | tf_op | source)
XLA Modules:
  0.0 198.4 jit_solution(15772310761905478033)
XLA Ops:
  0.6 191.1 %shard_map.50 = (f32[576,4608]{1,0:T(8,128)S(1)}, f32[576,1152]{1,0:T(8,128)S(1)}, f32[16,4608]{1,0:T(8,128)S(1)}, f32[576,128]{1,0:T(8,128)S(1)}, f32[8,128]{1,0:T(8,128)S(1)}) custom-call(bf16[128,4608]{1,0:T(8,128)(2,1)} %emb.1, s32[1,128]{1,0:T(1,128)} %bitcast.9, f32[576,1152]{1,0:T(8,128)} %bitcast.7), custom_call_target="tpu_custom_call" | custom-call | flops 12079595520 | bytes 41943040 | tf_op jit(solution)/shard_map/pallas_call | solution.py:499
  191.8 6.7 %shard_map.51 = (f32[576,4608]{1,0:T(8,128)}, f32[576,1152]{1,0:T(8,128)}) custom-call(f32[576,4608]{1,0:T(8,128)S(1)} %get-tuple-element.9.gram, f32[576,1152]{1,0:T(8,128)S(1)} %get-tuple-element.10.panel, f32[16,4608]{1,0:T(8,128)S(1)} %get-tuple-element.11.ssum, f32[576,128]{1,0:T(8,128)S(1)} %get-tuple-element.12.tsum, f32[8,128]{1,0:T(8,128)S(1)} %get-tuple-element.13.cnt), custom_call_target="tpu_custom_call" | custom-call | tf_op jit(solution)/shard_map/pallas_call | solution.py:559

commit v4 on v3

--- a/solution.py
+++ b/solution.py
@@ -162,39 +162,6 @@
     for d in (1, 2, 3):
         sig(c, at_x(d, zoff))
         sig(c, at_x(d, zmate))
-    pl.semaphore_wait(bar, 37)
-
-    def put(src, dst, dev, ssem, rsem):
-        pltpu.make_async_remote_copy(
-            src_ref=src, dst_ref=dst, send_sem=ssem, recv_sem=rsem, device_id=dev, device_id_type=MESH
-        ).start()
-
-    def wait(ref, sem):
-        pltpu.make_async_copy(ref, ref, sem).wait()
-
-    def put_same(ref, ff, ssem, rsem):
-        put(ref, ref, (c, ff), ssem, rsem)
-
-    def piece(j, i, lo=0, hi=COLS):
-        r = pl.multiple_of(COLS * j + PIECE[j] * i, 8)
-        return W.at[pl.ds(r, PIECE[j]), COLS * j + lo : COLS * j + hi]
-
-    for src in (0, 1):
-
-        @pl.when(f == src)
-        def _():
-            for j in range(NPAN):
-                for i in range(FEAT):
-                    r = COLS * j + PIECE[j] * i
-                    if r // OWN != src:
-                        continue
-                    r = r - OWN * src
-                    ref = prev.at[r : r + PIECE[j], COLS * j : COLS * (j + 1)]
-                    if i == src:
-                        pltpu.make_async_copy(ref, piece(j, i), lr.at[j]).start()
-                    else:
-                        put(ref, piece(j, i), (c, i), ls.at[j], lr.at[j])
-
     n = emb.shape[0]
     label = lab[...].astype(jnp.float32)
     onehot = (lax.broadcasted_iota(jnp.int32, (CLS, n), 0).astype(jnp.float32) == label).astype(jnp.float32)
@@ -210,11 +177,46 @@
     for i in range(CLS):
         CST[i] = jnp.broadcast_to(counts[i : i + 1, :], (8, 128))
     emb_copy.wait()
-    for ref, w, c0 in ((STQ, QW, PW), (STP, PW, 0)):
+
+    def choose(ref, w, c0):
         for i in range(w // 512):
             cols = slice(512 * i, 512 * (i + 1))
             chosen = jnp.dot(pick, E[:, c0 + 512 * i : c0 + 512 * (i + 1)], preferred_element_type=jnp.float32)
             ref[:, cols] = chosen.astype(jnp.bfloat16)
+
+    choose(STQ, QW, PW)
+    pl.semaphore_wait(bar, 37)
+
+    def put(src, dst, dev, ssem, rsem):
+        pltpu.make_async_remote_copy(
+            src_ref=src, dst_ref=dst, send_sem=ssem, recv_sem=rsem, device_id=dev, device_id_type=MESH
+        ).start()
+
+    def wait(ref, sem):
+        pltpu.make_async_copy(ref, ref, sem).wait()
+
+    def put_same(ref, ff, ssem, rsem):
+        put(ref, ref, (c, ff), ssem, rsem)
+
+    def piece(j, i, lo=0, hi=COLS):
+        r = pl.multiple_of(COLS * j + PIECE[j] * i, 8)
+        return W.at[pl.ds(r, PIECE[j]), COLS * j + lo : COLS * j + hi]
+
+    for src in (0, 1):
+
+        @pl.when(f == src)
+        def _():
+            for j in range(NPAN):
+                for i in range(FEAT):
+                    r = COLS * j + PIECE[j] * i
+                    if r // OWN != src:
+                        continue
+                    r = r - OWN * src
+                    ref = prev.at[r : r + PIECE[j], COLS * j : COLS * (j + 1)]
+                    if i == src:
+                        pltpu.make_async_copy(ref, piece(j, i), lr.at[j]).start()
+                    else:
+                        put(ref, piece(j, i), (c, i), ls.at[j], lr.at[j])
 
     def rows_of(ref, cc):
         return ref.at[pl.ds(pl.multiple_of(CAP * cc, CAP), CAP), :]
@@ -238,6 +240,7 @@
         return 0
 
     lax.fori_loop(0, CLS, route, 0)
+    choose(STP, PW, 0)
 
     def route_p(cc, _):
         same = lax.rem(cc // 2, 2) == zhi
@@ -398,27 +401,27 @@
             for i in range(n // 512):
                 chunk(i, 0)
 
-    lead_a(0)
+    for j in range(NPAN):
+        lead_a(j)
     lead_b(0)
     start_q()
     lead_c(0)
-    lead_a(1)
-    lead_a(2)
+    start_p()
     lead_d(0)
     own_copy.wait()
 
     events = {
-        0: [start_p],
-        1: [lambda: lead_b(1), lambda: lead_b(2)],
-        2: [lambda: lead_c(1), lambda: lead_c(2), count],
-        4: [lambda: lead_d(1), lambda: forward(0, False)],
-        5: [lambda: lead_d(2), lambda: forward(0, True)],
-        7: [start_mate_p],
-        8: [lambda: far_in(0)],
-        11: [lambda: mate_q(0)],
-        12: [lambda: forward(1, False)],
-        14: [lambda: forward(1, True)],
-        16: [lambda: forward(2, False)],
+        0: [lambda: lead_b(1), lambda: lead_b(2)],
+        1: [lambda: lead_c(1), lambda: lead_c(2), count],
+        3: [lambda: forward(0, False)],
+        4: [lambda: lead_d(1), lambda: forward(0, True)],
+        5: [lambda: lead_d(2)],
+        6: [start_mate_p],
+        7: [lambda: far_in(0)],
+        10: [lambda: mate_q(0)],
+        11: [lambda: forward(1, False)],
+        13: [lambda: forward(1, True)],
+        15: [lambda: forward(2, False)],
     }
 
     def hooks(k, place):

time: 199 us -> 194 us (0.975)
  Pallas kernels: 198 us -> 193 us
    pallas_call x1, Pallas kernels: 191 us -> 187 us  [exchange(): pl.pallas_call(kernel, out_shape=(pltpu.VMEM((TILE, D), jnp.float32), plt...]
where the time goes in v4:
time: 194 us
  Pallas kernels  193 us (99%)
    pallas_call x1, Pallas kernels, exchange(): pl.pallas_call(kernel, out_shape=(pltpu.VMEM((TILE, D), jnp.float32), plt...  187 us
    pallas_call x1, Pallas kernels, finish(): pl.pallas_call(finish_kernel, grid=(TILE // 64,), out_shape=(jax.ShapeDty...  6.66 us

profile of v4, /device:TPU:0, one launch (start us, length us, event | category | flops | bytes accessed | tf_op | source)
XLA Modules:
  0.0 194.1 jit_solution(17564813482662500974)
XLA Ops:
  0.6 186.8 %shard_map.50 = (f32[576,4608]{1,0:T(8,128)S(1)}, f32[576,1152]{1,0:T(8,128)S(1)}, f32[16,4608]{1,0:T(8,128)S(1)}, f32[576,128]{1,0:T(8,128)S(1)}, f32[8,128]{1,0:T(8,128)S(1)}) custom-call(bf16[128,4608]{1,0:T(8,128)(2,1)} %emb.1, s32[1,128]{1,0:T(1,128)} %bitcast.9, f32[576,1152]{1,0:T(8,128)} %bitcast.7), custom_call_target="tpu_custom_call" | custom-call | flops 12079595520 | bytes 41943040 | tf_op jit(solution)/shard_map/pallas_call | solution.py:502
  187.5 6.7 %shard_map.51 = (f32[576,4608]{1,0:T(8,128)}, f32[576,1152]{1,0:T(8,128)}) custom-call(f32[576,4608]{1,0:T(8,128)S(1)} %get-tuple-element.9.gram, f32[576,1152]{1,0:T(8,128)S(1)} %get-tuple-element.10.panel, f32[16,4608]{1,0:T(8,128)S(1)} %get-tuple-element.11.ssum, f32[576,128]{1,0:T(8,128)S(1)} %get-tuple-element.12.tsum, f32[8,128]{1,0:T(8,128)S(1)} %get-tuple-element.13.cnt), custom_call_target="tpu_custom_call" | custom-call | tf_op jit(solution)/shard_map/pallas_call | solution.py:562
